TPU v7x, 128 devices: a whole 4x4x4 slice. The times are simulated.
128 devices in a mesh: grp: 4 (over y_hi, core), blk: 32 (over y_lo, x, z).
Axes of the slice: x: 4, y: 4 (y_hi: 2, y_lo: 2; y = y_hi * 2 + y_lo), z: 4, core: 2. Of those that a mesh axis runs over, the one named last changes fastest.
Arguments:
- queries: bfloat16 [5376, 2048], P('blk', 'grp'), may hold values from -512 to 512
- key_rows: bfloat16 [5376, 2048], P('blk', 'grp'), may hold values from -8 to 8
- value_rows: bfloat16 [5376, 2048], P('blk', 'grp'), may hold values from -6 to 6
- out_grad: bfloat16 [5376, 2048], P('blk', 'grp'), may hold values from -6 to 6
- enc_lengths: int32 [32], P('blk'), may hold values from 42 to 168, as said below
- dec_lengths: int32 [32], P('blk'), may hold values from 14 to 56, as said below
Outputs:
- query_grad: float32 [5376, 2048], P('blk', 'grp')
- key_grad: float32 [5376, 2048], P('blk', 'grp')
- value_grad: float32 [5376, 2048], P('blk', 'grp')
Inputs may be any that keep to these rules, and one draw needn't show every extreme that they name: `enc_lengths`: some encoder block is full. `dec_lengths`: some decoder block is full.
All inputs are finite; a program needn't handle non-finite values.
Results may differ from a plain program's by a relative error of at most 0.0055.
Values may be sent and summed in bfloat16 or wider, within the bound.
No kernel may reach another device: no remote copies, remote signals or barrier semaphores. Data moves between devices by JAX's collectives and lax.ppermute only.
A program may use at most 128 MiB of HBM per device.

v0:
```python
import functools

import jax
import jax.numpy as jnp
from jax import lax
from jax.experimental import pallas as pl
from jax.experimental.pallas import tpu as pltpu
from jax.sharding import PartitionSpec as P

HD = 64
LANES = 128
NB = 32
TOK = 168
DTOK = 56
QTR = TOK // 4
DQTR = DTOK // 4
IN_ROWS = 216
DIN_ROWS = 72
OUT_ROWS = 192
DOUT_ROWS = 64
NQ_ENC = NB * QTR
DQ = NB * DQTR
TQ = 256
TK = 2048
SUB = 256
TKD = 768
NK_ENC = -(-(NB * 176) // TK) * TK
NK_DEC = -(-(NB * 64) // TKD) * TKD
REST = 2 * TQ - DQ
FIRST_TILES = 3
LAST_TILES = (NQ_ENC - REST) // TQ - FIRST_TILES
THERE_ROWS = 2 * TQ + 48
BACK_ROWS = 2 * TQ + 32
NEG = -1e30
F32 = jnp.float32
BF16 = jnp.bfloat16
MIB = 1024 * 1024


def flip(head):
    return (head + 4) % 8


def lane_low(shape):
    return lax.broadcasted_iota(jnp.int32, shape, len(shape) - 1) < HD


def pair_up(first, second):
    low = lane_low(first.shape)
    even = jnp.where(low, first, pltpu.roll(second, HD, 1))
    odd = jnp.where(low, pltpu.roll(first, HD, 1), second)
    return even, odd


def pack_kernel(group_ref, part_ref, enc_ref, dec_ref, q_in, k_in, v_in, g_in, x_out,
                q_ref, k_ref, v_ref, g_ref, kv_s, qg_s, x_ref, in_sem, out_sem):
    is_dec = group_ref[0] == 3
    arrays = ((k_in, k_ref), (v_in, v_ref), (q_in, q_ref), (g_in, g_ref))
    fetches = [
        [
            pltpu.make_async_copy(src.at[:, pl.ds(pair * LANES, LANES)], dst.at[pair], in_sem.at[pair, i])
            for i, (src, dst) in enumerate(arrays)
        ]
        for pair in range(4)
    ]
    for some in fetches:
        for copy in some:
            copy.start()
    row = lax.broadcasted_iota(jnp.int32, (8, LANES), 0)
    enc_len, dec_len = enc_ref[0].astype(F32), dec_ref[0].astype(F32)
    tail = jnp.where(row == 6, enc_len, jnp.where(row == 7, dec_len, 0.0))

    def sent(pair):
        some = pl.ds(8 * pair, 8)
        return pltpu.make_async_copy(x_ref.at[some], x_out.at[some], out_sem.at[pair])

    for pair in range(4):
        for copy in fetches[pair]:
            copy.wait()
        even, odd = pair_up(k_ref[pair].astype(F32), v_ref[pair].astype(F32))
        kv_s[2 * pair], kv_s[2 * pair + 1] = even, odd
        even, odd = pair_up(q_ref[pair].astype(F32), g_ref[pair].astype(F32))
        qg_s[2 * pair], qg_s[2 * pair + 1] = even, odd

        @pl.when(jnp.logical_not(is_dec))
        def _():
            for head in (2 * pair, 2 * pair + 1):
                kv = kv_s[head]
                for part in range(4):
                    qg = qg_s[head, pl.ds(part * QTR, QTR), :]
                    x_ref[4 * head + part] = jnp.concatenate([kv, qg, tail[2:]], axis=0).astype(BF16)
            sent(pair).start()

    @pl.when(is_dec)
    def _():
        for head in range(8):
            for part in range(4):
                pieces = []
                for c in range(3):
                    src = flip(head) if c < 2 else head
                    pieces.append(kv_s[src, pl.ds(c, DTOK, stride=3), :])
                    pieces.append(qg_s[src, pl.ds(3 * part * DQTR + c, DQTR, stride=3), :])
                    pieces.append(tail[6:])
                x_ref[4 * head + part] = jnp.concatenate(pieces, axis=0).astype(BF16)
            if head % 2 == 1:
                sent(head // 2).start()

    for pair in range(4):
        sent(pair).wait()


def unpack_kernel(group_ref, w_ref, qo_ref, ko_ref, vo_ref, dq_s, dk_s, dv_s, tmp_s):
    is_dec = group_ref[0] == 3

    @pl.when(jnp.logical_not(is_dec))
    def _():
        for pair in range(4):
            cols = pl.ds(pair * LANES, LANES)
            sums = []
            for head in (2 * pair, 2 * pair + 1):
                total = None
                for part in range(4):
                    chunk = w_ref[4 * head + part].astype(F32)
                    total = chunk[:TOK] if total is None else total + chunk[:TOK]
                    dq = chunk[TOK:]
                    turned = pltpu.roll(dq, HD, 1)
                    first, second = (dq, turned) if head % 2 == 0 else (turned, dq)
                    base = part * QTR
                    if head % 2 == 0:
                        dq_s[pl.ds(base, 21), :] = first[:21]
                        dq_s[pl.ds(base + 21, 21), :] = second[:21]
                    else:
                        low = lane_low((21, LANES))
                        for start, value in ((base, first), (base + 21, second)):
                            old = dq_s[pl.ds(start, 21), :]
                            dq_s[pl.ds(start, 21), :] = jnp.where(low, old, value[:21])
                sums.append(total)
            low = lane_low((TOK, LANES))
            ko_ref[:, cols] = jnp.where(low, sums[0], pltpu.roll(sums[1], HD, 1))
            vo_ref[:, cols] = jnp.where(low, pltpu.roll(sums[0], HD, 1), sums[1])
            qo_ref[:, cols] = dq_s[...]

    @pl.when(is_dec)
    def _():
        for pair in range(4):
            cols = pl.ds(pair * LANES, LANES)
            for c in range(3):
                sums, dqs = [], []
                for head in (2 * pair, 2 * pair + 1):
                    place = flip(head) if c < 2 else head
                    total, pieces = None, []
                    for part in range(4):
                        chunk = w_ref[4 * place + part].astype(F32)[DOUT_ROWS * c : DOUT_ROWS * (c + 1)]
                        kv = chunk[:DTOK]
                        total = kv if total is None else total + kv
                        dq = chunk[DTOK:]
                        turned = pltpu.roll(dq, HD, 1)
                        pieces.append((dq, turned) if head % 2 == 0 else (turned, dq))
                    sums.append(total)
                    dqs.append(pieces)
                low = lane_low((DTOK, LANES))
                rows = pl.ds(c, DTOK, stride=3)
                dk_s[rows, :] = jnp.where(low, sums[0], pltpu.roll(sums[1], HD, 1))
                dv_s[rows, :] = jnp.where(low, pltpu.roll(sums[0], HD, 1), sums[1])
                low = lane_low((8, LANES))
                for part in range(4):
                    for half in range(2):
                        value = jnp.where(low, dqs[0][part][half], dqs[1][part][half])
                        tmp_s[pl.ds(part * DQTR + half * 7, 7), :] = value[:7]
                dq_s[rows, :] = tmp_s[...]
            ko_ref[:, cols] = dk_s[...]
            vo_ref[:, cols] = dv_s[...]
            qo_ref[:, cols] = dq_s[...]


def fold(tile, op):
    parts = [tile[8 * i : 8 * i + 8] for i in range(tile.shape[0] // 8)]
    while len(parts) > 1:
        parts = [op(parts[i], parts[i + 1]) if i + 1 < len(parts) else parts[i] for i in range(0, len(parts), 2)]
    return parts[0]


def spread(stat, rows):
    return jnp.concatenate([stat] * (rows // 8), axis=0)


def tile_rows(kt, size):
    return pl.ds(pl.multiple_of(kt * size, size), size)


def place_block(kv_ref, ka_ref, block, offset, length):
    size = block.shape[0]
    row = lax.broadcasted_iota(jnp.int32, (size, LANES), 0)
    lane = lax.broadcasted_iota(jnp.int32, (size, LANES), 1)
    rows = pl.ds(pl.multiple_of(offset, 16), size)
    kv_ref[rows, :] = block
    bias = jnp.where(row < length, 0.0, NEG)
    ka_ref[rows, :] = jnp.where(lane == HD, bias, block.astype(F32)).astype(BF16)


def place_padding(kv_ref, ka_ref, offset, size):
    lane = lax.broadcasted_iota(jnp.int32, (size, LANES), 1)
    rows = pl.ds(pl.multiple_of(offset, 16), size)
    kv_ref[rows, :] = jnp.zeros((size, LANES), BF16)
    ka_ref[rows, :] = jnp.where(lane == HD, NEG, 0.0).astype(BF16)


def turn(keys):
    return keys.astype(F32).T[:HD].astype(BF16)


def read_lens(y_ref, wide_s, lens_s, sem):
    lane = lax.broadcasted_iota(jnp.int32, (8, LANES), 1)
    found = jnp.zeros((8, LANES), F32)
    for b in range(NB):
        found = jnp.where(lane == b, y_ref[b].astype(F32)[IN_ROWS - 8 :], found)
    wide_s[...] = found.astype(jnp.int32)
    copy = pltpu.make_async_copy(wide_s, lens_s, sem)
    copy.start()
    copy.wait()


def query_operands(qg):
    turned = qg.T
    sub = lax.broadcasted_iota(jnp.int32, (LANES, TQ), 0)
    q_t = jnp.where(sub < HD, turned * 0.125, jnp.where(sub == HD, 1.0, 0.0)).astype(BF16)
    d_t = jnp.where(sub < HD, 0.0, turned).astype(BF16)
    return q_t, d_t


def natural_operands(qg):
    low = lane_low((TQ, LANES))
    return jnp.where(low, qg, 0.0).astype(BF16), jnp.where(low, 0.0, qg).astype(BF16)


def score_sums(found, running):
    s, dprob = found
    peak, norm, inner = running
    new_peak = jnp.maximum(peak, fold(s, jnp.maximum))
    prob = jnp.exp(s - spread(new_peak, s.shape[0]))
    shrink = jnp.exp(peak - new_peak)
    norm = norm * shrink + fold(prob, jnp.add)
    inner = inner * shrink + fold(prob * dprob, jnp.add)
    return new_peak, norm, inner


def merged(running):
    peak8, norm8, inner8 = running
    peak = jnp.max(peak8, axis=0, keepdims=True)
    shrink = jnp.exp(peak8 - peak)
    norm = jnp.sum(norm8 * shrink, axis=0, keepdims=True)
    inner = jnp.sum(inner8 * shrink, axis=0, keepdims=True)
    return peak, norm, inner


def no_moments():
    zero = jnp.zeros((8, TQ), F32)
    return jnp.full((8, TQ), NEG, F32), zero, zero


def grad_parts(s, dprob, total, delta):
    prob = jnp.exp(s - total)
    dscore = (prob * (dprob - delta)).astype(BF16)
    return prob.astype(BF16), dscore


def key_grads(parts, naturals):
    prob, dscore = parts
    q_nat, d_nat = naturals
    return jnp.dot(dscore, q_nat, preferred_element_type=F32) + jnp.dot(
        prob, d_nat, preferred_element_type=F32
    )


def both_halves(dq_t):
    dq_t = dq_t * 0.125
    return jnp.concatenate([dq_t, dq_t], axis=0).T


def write_split(ref, first_row, value):
    for term in range(3):
        low = value.astype(BF16).astype(F32)
        value = value - low
        for half in range(2):
            ref[pl.ds(first_row + 4 * term + half, 1), :] = low[:, half * LANES : (half + 1) * LANES]


def read_split(rows, first_row):
    total = None
    for term in (2, 1, 0):
        at = first_row + 4 * term
        piece = jnp.concatenate([rows[at : at + 1], rows[at + 1 : at + 2]], axis=1)
        total = piece if total is None else total + piece
    return total


def sweep(count, tiles, refs, query, start, emit, arrive, ready, leave):
    kv_ref, ka_ref, kt_ref, acc_ref, s_pair, dp_pair = refs

    def tile_step(kt, slot, now, then, dq_t, running):
        found = None
        for j in range(TK // SUB):
            rows = pl.ds(pl.multiple_of(kt * TK + j * SUB, SUB), SUB)
            fresh = None
            if then is not None:
                q_t, d_t = then
                fresh = (
                    jnp.dot(ka_ref[rows, :], q_t, preferred_element_type=F32),
                    jnp.dot(kv_ref[rows, :], d_t, preferred_element_type=F32),
                )
                s_pair[1 - slot][rows, :], dp_pair[1 - slot][rows, :] = fresh
            if now is not None:
                naturals, total, delta = now
                parts = grad_parts(s_pair[slot][rows, :], dp_pair[slot][rows, :], total, delta)
            if found is not None:
                running = score_sums(found, running)
            if now is not None:
                acc_ref[rows, :] += key_grads(parts, naturals)
                keys = kt_ref[kt, :, j * SUB : (j + 1) * SUB]
                dq_t = dq_t + jnp.dot(keys, parts[1], preferred_element_type=F32)
            found = fresh
        if found is not None:
            running = score_sums(found, running)
        return dq_t, running

    def run(slot, now, then, running):
        def step(kt, carry):
            if now is None:
                arrive(kt)
            carry = tile_step(kt, slot, now, then, *carry)
            if then is None:
                leave(kt)
            return carry

        return lax.fori_loop(0, tiles, step, (jnp.zeros((HD, TQ), F32), running))

    _, running = run(1, None, query_operands(query(0)), start(0))
    ready()
    for t in range(count):
        peak, norm, inner = merged(running)
        total, delta = peak + jnp.log(norm), inner / norm
        now = natural_operands(query(t)), total, delta
        if t == count - 1:
            dq_t, _ = run(t % 2, now, None, no_moments())
        else:
            dq_t, running = run(t % 2, now, query_operands(query(t + 1)), start(t + 1))
        emit(t, dq_t, total, delta)


def tile_copy(src_ref, dst_ref, sem, kt):
    rows = tile_rows(kt, TK)
    return pltpu.make_async_copy(src_ref.at[rows, :], dst_ref.at[rows, :], sem.at[kt])


def enc_first_kernel(group_ref, y_ref, kv_ref, ka_ref, kt_ref, qg_ref, acc_ref, dq_ref, meta_ref,
                     kv_s, ka_s, kt_s, qg_s, acc_s, dq_s, s0_s, s1_s, dp0_s, dp1_s,
                     acc_sem, sems, wide_s, lens_s, sem):
    @pl.when(group_ref[0] < 3)
    def _():
        read_lens(y_ref, wide_s, lens_s, sem)

        def block(b, offset):
            length = lens_s[6, b]
            meta_ref[b] = offset
            meta_ref[NB + b] = length
            place_block(kv_s, ka_s, y_ref[b, 0:176, :], offset, length)
            return offset + ((length + 15) // 16) * 16

        end = lax.fori_loop(0, NB, block, jnp.int32(0))
        place_padding(kv_s, ka_s, end, TK)
        tiles = (end + TK - 1) // TK
        meta_ref[2 * NB] = tiles
        for b in range(NB):
            qg_s[pl.ds(QTR * b, 48), :] = y_ref[b].astype(F32)[TOK:]

        def arrive(kt):
            kt_s[kt] = turn(kv_s[tile_rows(kt, TK), :])
            acc_s[tile_rows(kt, TK), :] = jnp.zeros((TK, LANES), F32)

        copies = [
            pltpu.make_async_copy(src, dst, sems.at[i])
            for i, (src, dst) in enumerate(
                ((kv_s, kv_ref), (ka_s, ka_ref), (qg_s, qg_ref), (kt_s, kt_ref), (dq_s, dq_ref)))
        ]
        for copy in copies[:3]:
            copy.start()

        def emit(t, dq_t, total, delta):
            dq_s[pl.ds(t * TQ, TQ), :] = both_halves(dq_t)

        sweep(FIRST_TILES, tiles, (kv_s, ka_s, kt_s, acc_s, (s0_s, s1_s), (dp0_s, dp1_s)),
              lambda t: qg_s[pl.ds(t * TQ, TQ), :], lambda t: no_moments(), emit,
              arrive, copies[3].start, lambda kt: tile_copy(acc_s, acc_ref, acc_sem, kt).start())
        copies[4].start()
        for copy in copies:
            copy.wait()

        @pl.loop(0, tiles)
        def _(kt):
            tile_copy(acc_s, acc_ref, acc_sem, kt).wait()


def fetch_keys(tiles, kv, ka, kt_all, acc, kt_sem):
    @pl.loop(0, tiles)
    def _(kt):
        tile_copy(*kv, kt).start()
        tile_copy(*ka, kt).start()

    kt_copy = pltpu.make_async_copy(*kt_all, kt_sem)
    kt_copy.start()

    @pl.loop(0, tiles)
    def _(kt):
        tile_copy(*acc, kt).start()

    def arrive(kt):
        tile_copy(*kv, kt).wait()
        tile_copy(*ka, kt).wait()

    def ready():
        kt_copy.wait()

        @pl.loop(0, tiles)
        def _(kt):
            tile_copy(*acc, kt).wait()

    return arrive, ready


def enc_dec_kernel(group_ref, meta_ref, kv_ref, ka_ref, kt_ref, qg_ref, acc1_ref, m0_ref, m1_ref, m2_ref,
                   acc_ref, dq_ref, back_ref, kv_s, ka_s, kt_s, acc_s, s0_s, s1_s, dp0_s, dp1_s,
                   own_s, got_s, stat_s, kv_sem, ka_sem, acc_sem, out_sem, sems):
    group = group_ref[0]

    @pl.when(group < 3)
    def _():
        for c, m_ref in enumerate((m0_ref, m1_ref, m2_ref)):
            @pl.when(group == c)
            def _():
                pltpu.make_async_copy(m_ref, got_s, sems.at[0]).start()

        rest = pltpu.make_async_copy(
            qg_ref.at[pl.ds(NQ_ENC - REST, REST), :], own_s.at[pl.ds(DQ, REST), :], sems.at[1])
        rest.start()
        tiles = meta_ref[2 * NB]
        arrive, ready = fetch_keys(tiles, (kv_ref, kv_s, kv_sem), (ka_ref, ka_s, ka_sem), (kt_ref, kt_s),
                                   (acc1_ref, acc_s, acc_sem), sems.at[2])
        pltpu.make_async_copy(m0_ref, got_s, sems.at[0]).wait()
        got = got_s[...].astype(F32)
        own_s[pl.ds(0, DQ), :] = got[:DQ]
        stats = got[2 * TQ :]
        rest.wait()

        def start(t):
            row = lax.broadcasted_iota(jnp.int32, (8, TQ), 0)
            peak, norm, inner = (read_split(stats, 12 * k + 2 * t) for k in range(3))
            return (jnp.where(row == 0, peak, NEG), jnp.where(row == 0, norm, 0.0),
                    jnp.where(row == 0, inner, 0.0))

        stat_s[...] = jnp.zeros_like(stat_s)

        def emit(t, dq_t, total, delta):
            dq = both_halves(dq_t)
            back_ref[pl.ds(t * TQ, TQ), :] = dq.astype(BF16)
            write_split(stat_s, 2 * t, total)
            write_split(stat_s, 12 + 2 * t, delta)
            if t == 1:
                dq_ref[...] = dq[TQ - REST :]

        sweep(2, tiles, (kv_s, ka_s, kt_s, acc_s, (s0_s, s1_s), (dp0_s, dp1_s)),
              lambda t: own_s[pl.ds(t * TQ, TQ), :], start, emit,
              arrive, ready, lambda kt: tile_copy(acc_s, acc_ref, out_sem, kt).start())
        back_ref[pl.ds(2 * TQ, BACK_ROWS - 2 * TQ), :] = stat_s[...].astype(BF16)

        @pl.loop(0, tiles)
        def _(kt):
            tile_copy(acc_s, acc_ref, out_sem, kt).wait()


def enc_last_kernel(group_ref, meta_ref, kv_ref, ka_ref, kt_ref, qg_ref, acc2_ref, dq1_ref, dq2_ref,
                    o_ref, same_ref, kv_s, ka_s, kt_s, acc_s, s0_s, s1_s, dp0_s, dp1_s,
                    qg_s, dq_s, out_s, kv_sem, ka_sem, acc_sem, out_sem, sems):
    @pl.when(group_ref[0] < 3)
    def _():
        tiles = meta_ref[2 * NB]
        own = pltpu.make_async_copy(
            qg_ref.at[pl.ds(FIRST_TILES * TQ, LAST_TILES * TQ), :], qg_s, sems.at[0])
        own.start()
        arrive, ready = fetch_keys(tiles, (kv_ref, kv_s, kv_sem), (ka_ref, ka_s, ka_sem), (kt_ref, kt_s),
                                   (acc2_ref, acc_s, acc_sem), sems.at[1])
        early = [
            pltpu.make_async_copy(dq1_ref, dq_s.at[pl.ds(0, FIRST_TILES * TQ), :], sems.at[2]),
            pltpu.make_async_copy(dq2_ref, dq_s.at[pl.ds(NQ_ENC - REST, REST), :], sems.at[3]),
        ]
        for copy in early:
            copy.start()
        dq_s[pl.ds(NQ_ENC, 8), :] = jnp.zeros((8, LANES), F32)
        own.wait()

        def emit(t, dq_t, total, delta):
            dq_s[pl.ds((FIRST_TILES + t) * TQ, TQ), :] = both_halves(dq_t)

        sweep(LAST_TILES, tiles, (kv_s, ka_s, kt_s, acc_s, (s0_s, s1_s), (dp0_s, dp1_s)),
              lambda t: qg_s[pl.ds(t * TQ, TQ), :], lambda t: no_moments(), emit,
              arrive, ready, lambda kt: None)
        for copy in early:
            copy.wait()
        row = lax.broadcasted_iota(jnp.int32, (TOK, LANES), 0)
        low = lane_low((TOK, LANES))
        copies = []
        for b in range(NB):
            grad = acc_s[pl.ds(pl.multiple_of(meta_ref[b], 16), TOK), :]
            grad = jnp.where(row < meta_ref[NB + b], jnp.where(low, grad * 0.125, grad), 0.0)
            base = QTR * b
            dq = jnp.where(lane_low((24, LANES)), dq_s[pl.ds(base, 24), :], dq_s[pl.ds(base + 21, 24), :])
            out_s[b] = jnp.concatenate([grad, dq], axis=0).astype(BF16)
            if b % 8 == 7:
                some = pl.ds(b - 7, 8)
                copies.append(pltpu.make_async_copy(out_s.at[some], o_ref.at[some], out_sem.at[b // 8]))
                copies[-1].start()
        for copy in copies:
            copy.wait()


def dec_query_pos(t, part):
    q_id = t * TQ + lax.broadcasted_iota(jnp.int32, (1, TQ), 1)
    place = (q_id // DQTR) * DTOK + part * DQTR + q_id % DQTR
    return jnp.where(q_id < DQ, place, -1).astype(F32)


def dec_scores(kv_ref, ka_ref, pos_ref, c, rows, operands, q_at):
    q_t, d_t = operands
    s = jnp.dot(ka_ref[c, rows, :], q_t, preferred_element_type=F32)
    dprob = jnp.dot(kv_ref[c, rows, :], d_t, preferred_element_type=F32)
    k_at = pos_ref[rows, :]
    return jnp.where(jnp.concatenate([k_at, k_at], axis=1) <= q_at, s, NEG), dprob


def put_pos(pos_ref, offset, b):
    row = lax.broadcasted_iota(jnp.int32, (64, LANES), 0)
    pos_ref[pl.ds(pl.multiple_of(offset, 16), 64), :] = (row + b * DTOK).astype(F32)


def dec_units(kt):
    return [
        (pl.ds(pl.multiple_of(kt * TKD + j * SUB, SUB), SUB), t) for j in range(TKD // SUB) for t in range(2)
    ]


def dec_first_kernel(group_ref, part_ref, held_ref, kv_out, ka_out, kt_out, m0_out, m1_out, m2_out, meta_ref,
                     y_ref, kv_ref, ka_ref, kt_ref, pos_ref, m_ref, qg_s, stat_s, sems, wide_s, lens_s, sem):
    @pl.when(group_ref[0] == 3)
    def _():
        fetch = pltpu.make_async_copy(held_ref, y_ref, sems.at[0])
        fetch.start()
        fetch.wait()
        read_lens(y_ref, wide_s, lens_s, sem)

        def block(b, offset):
            length = lens_s[7, b]
            meta_ref[b] = offset
            meta_ref[NB + b] = length
            chunk = y_ref[b].astype(F32)
            for c in range(3):
                keys = chunk[DIN_ROWS * c : DIN_ROWS * c + 64].astype(BF16)
                place_block(kv_ref.at[c], ka_ref.at[c], keys, offset, length)
            put_pos(pos_ref, offset, b)
            return offset + ((length + 15) // 16) * 16

        end = lax.fori_loop(0, NB, block, jnp.int32(0))
        for c in range(3):
            place_padding(kv_ref.at[c], ka_ref.at[c], end, TKD)
        tiles = (end + TKD - 1) // TKD
        meta_ref[2 * NB] = tiles
        for b in range(NB):
            chunk = y_ref[b].astype(F32)
            for c in range(3):
                qg_s[c, pl.ds(DQTR * b, 16), :] = chunk[DIN_ROWS * c + DTOK : DIN_ROWS * (c + 1)]
        part = part_ref[0]
        stat_s[...] = jnp.zeros_like(stat_s)
        for c in range(3):
            qg_s[c, pl.ds(DQ, REST), :] = jnp.zeros((REST, LANES), F32)
            m_ref[c, pl.ds(0, 2 * TQ), :] = qg_s[c].astype(BF16)

            @pl.loop(0, tiles)
            def _(kt):
                kt_ref[c, kt] = turn(kv_ref[c, tile_rows(kt, TKD), :])

        copies = [
            pltpu.make_async_copy(src, dst, sems.at[1 + i])
            for i, (src, dst) in enumerate(
                ((kv_ref, kv_out), (ka_ref, ka_out), (kt_ref, kt_out)))
        ]
        for copy in copies:
            copy.start()
        for c, out in enumerate((m0_out, m1_out, m2_out)):
            operands = [query_operands(qg_s[c, pl.ds(t * TQ, TQ), :]) for t in range(2)]
            q_at = [dec_query_pos(t, part) for t in range(2)]

            def step(kt, carry):
                carry = list(carry)
                units = dec_units(kt)
                ahead = lambda u: dec_scores(kv_ref, ka_ref, pos_ref, c, units[u][0], operands[units[u][1]], q_at[units[u][1]])
                found = ahead(0)
                for u, (rows, t) in enumerate(units):
                    fresh = ahead(u + 1) if u + 1 < len(units) else None
                    carry[t] = score_sums(found, carry[t])
                    found = fresh
                return tuple(carry)

            found = lax.fori_loop(0, tiles, step, (no_moments(), no_moments()))
            for t in range(2):
                q_id = t * TQ + lax.broadcasted_iota(jnp.int32, (1, TQ), 1)
                for k, value in enumerate(merged(found[t])):
                    write_split(stat_s, 12 * k + 2 * t, jnp.where(q_id < DQ, value, NEG if k == 0 else 0.0))
            m_ref[c, pl.ds(2 * TQ, THERE_ROWS - 2 * TQ), :] = stat_s[...].astype(BF16)
            copies.append(pltpu.make_async_copy(m_ref.at[c], out, sems.at[4 + c]))
            copies[-1].start()
        for copy in copies:
            copy.wait()


def dec_last_kernel(group_ref, part_ref, meta_ref, kv_in, ka_in, kt_in, m0_in, m1_in, m2_in, b0_in, b1_in, b2_in, enc_ref,
                    o_ref, kv_ref, ka_ref, kt_ref, pos_ref, m_ref, back_ref, acc_s, dq_s, out_s, sems, sem):
    @pl.when(group_ref[0] == 3)
    def _():
        tiles = meta_ref[2 * NB]
        part = part_ref[0]
        fetches = [
            [
                pltpu.make_async_copy(src, dst.at[c], sems.at[c, i])
                for i, (src, dst) in enumerate(
                    ((m_in, m_ref), (b_in, back_ref), (kv_in.at[c], kv_ref), (ka_in.at[c], ka_ref), (kt_in.at[c], kt_ref)))
            ]
            for c, (m_in, b_in) in enumerate(((m0_in, b0_in), (m1_in, b1_in), (m2_in, b2_in)))
        ]
        for some in fetches:
            for copy in some:
                copy.start()

        @pl.loop(0, NB)
        def _(b):
            put_pos(pos_ref, meta_ref[b], b)

        for c in range(3):
            for copy in fetches[c]:
                copy.wait()
            qg = m_ref[c, pl.ds(0, 2 * TQ), :].astype(F32)
            back = back_ref[c].astype(F32)
            stats = back[2 * TQ :]
            cut = [qg[t * TQ : (t + 1) * TQ] for t in range(2)]
            operands = [query_operands(cut[t]) for t in range(2)]
            naturals = [natural_operands(cut[t]) for t in range(2)]
            q_at = [dec_query_pos(t, part) for t in range(2)]
            total = [read_split(stats, 2 * t) for t in range(2)]
            delta = [read_split(stats, 12 + 2 * t) for t in range(2)]

            def step(kt, dqs):
                dqs = list(dqs)
                units = dec_units(kt)
                ahead = lambda u: dec_scores(kv_ref, ka_ref, pos_ref, c, units[u][0], operands[units[u][1]], q_at[units[u][1]])
                found = ahead(0)
                for u, (rows, t) in enumerate(units):
                    fresh = ahead(u + 1) if u + 1 < len(units) else None
                    parts = grad_parts(*found, total[t], delta[t])
                    grad = key_grads(parts, naturals[t])
                    acc_s[rows, :] = grad if t == 0 else acc_s[rows, :] + grad
                    keys = kt_ref[c, kt, :, u // 2 * SUB : (u // 2 + 1) * SUB]
                    dqs[t] = dqs[t] + jnp.dot(keys, parts[1], preferred_element_type=F32)
                    found = fresh
                return tuple(dqs)

            none = jnp.zeros((HD, TQ), F32)
            dqs = lax.fori_loop(0, tiles, step, (none, none))
            for t in range(2):
                rows = pl.ds(t * TQ, TQ)
                dq_s[rows, :] = both_halves(dqs[t]) + back[t * TQ : (t + 1) * TQ]
            row = lax.broadcasted_iota(jnp.int32, (DTOK, LANES), 0)
            low = lane_low((DTOK, LANES))
            for b in range(NB):
                grad = acc_s[pl.ds(pl.multiple_of(meta_ref[b], 16), DTOK), :]
                grad = jnp.where(row < meta_ref[NB + b], jnp.where(low, grad * 0.125, grad), 0.0)
                base = DQTR * b
                dq = jnp.where(lane_low((8, LANES)), dq_s[pl.ds(base, 8), :], dq_s[pl.ds(base + 7, 8), :])
                out_s[b, pl.ds(DOUT_ROWS * c, DOUT_ROWS), :] = jnp.concatenate([grad, dq], axis=0).astype(BF16)
        copy = pltpu.make_async_copy(out_s, o_ref, sem)
        copy.start()
        copy.wait()


SMEM = pl.BlockSpec(memory_space=pltpu.SMEM)
VMEM = pl.BlockSpec(memory_space=pltpu.VMEM)
ANY = pl.BlockSpec(memory_space=pl.ANY)


def limit(mib):
    return pltpu.CompilerParams(vmem_limit_bytes=mib * MIB)


def shaped(shape, dtype):
    return jax.ShapeDtypeStruct(shape, dtype)


def lens_scratch():
    return [
        pltpu.VMEM((8, LANES), jnp.int32),
        pltpu.SMEM((8, LANES), jnp.int32),
        pltpu.SemaphoreType.DMA(()),
    ]


def key_scratch():
    return [
        pltpu.VMEM((NK_ENC + TK, LANES), BF16),
        pltpu.VMEM((NK_ENC + TK, LANES), BF16),
        pltpu.VMEM((NK_ENC // TK, HD, TK), BF16),
    ]


def score_scratch():
    return [pltpu.VMEM((NK_ENC, LANES), F32)] + [pltpu.VMEM((NK_ENC, TQ), F32)] * 4


def dma(*shape):
    return pltpu.SemaphoreType.DMA(shape)


META = shaped((2 * NB + 8,), jnp.int32)
ENC_TILES = NK_ENC // TK


def dec_first(group, part, held):
    keys = [((3, NK_DEC + TKD, LANES), BF16), ((3, NK_DEC + TKD, LANES), BF16),
            ((3, NK_DEC // TKD, HD, TKD), BF16)]
    pos = ((NK_DEC + TKD, LANES), F32)
    return pl.pallas_call(
        dec_first_kernel,
        out_shape=[shaped(*k) for k in keys] + [shaped((THERE_ROWS, LANES), BF16)] * 3 + [META],
        in_specs=[SMEM, SMEM, ANY],
        out_specs=[ANY] * 6 + [SMEM],
        scratch_shapes=[pltpu.VMEM(held.shape, BF16)] + [pltpu.VMEM(*k) for k in keys + [pos]] + [
            pltpu.VMEM((3, THERE_ROWS, LANES), BF16),
            pltpu.VMEM((3, 2 * TQ, LANES), F32),
            pltpu.VMEM((THERE_ROWS - 2 * TQ, LANES), F32),
            dma(8),
        ] + lens_scratch(),
        compiler_params=limit(24),
    )(group, part, held)


def enc_first(group, held):
    return pl.pallas_call(
        enc_first_kernel,
        out_shape=[
            shaped((NK_ENC + TK, LANES), BF16),
            shaped((NK_ENC + TK, LANES), BF16),
            shaped((ENC_TILES, HD, TK), BF16),
            shaped((NQ_ENC + 8, LANES), F32),
            shaped((NK_ENC, LANES), F32),
            shaped((FIRST_TILES * TQ, LANES), F32),
            META,
        ],
        in_specs=[SMEM, VMEM],
        out_specs=[ANY] * 6 + [SMEM],
        scratch_shapes=key_scratch() + [
            pltpu.VMEM((NQ_ENC + 8, LANES), F32),
            score_scratch()[0],
            pltpu.VMEM((FIRST_TILES * TQ, LANES), F32),
        ] + score_scratch()[1:] + [dma(ENC_TILES), dma(5)] + lens_scratch(),
        compiler_params=limit(38),
    )(group, held)


def enc_dec(group, meta, keys, acc, messages):
    return pl.pallas_call(
        enc_dec_kernel,
        out_shape=[
            shaped((NK_ENC, LANES), F32),
            shaped((REST, LANES), F32),
            shaped((BACK_ROWS, LANES), BF16),
        ],
        in_specs=[SMEM, SMEM] + [ANY] * 8,
        out_specs=[ANY, VMEM, VMEM],
        scratch_shapes=key_scratch() + score_scratch() + [
            pltpu.VMEM((2 * TQ, LANES), F32),
            pltpu.VMEM((THERE_ROWS, LANES), BF16),
            pltpu.VMEM((BACK_ROWS - 2 * TQ, LANES), F32),
            dma(ENC_TILES), dma(ENC_TILES), dma(ENC_TILES), dma(ENC_TILES), dma(3),
        ],
        input_output_aliases={6: 0},
        compiler_params=limit(38),
    )(group, meta, *keys, acc, *messages)


def enc_last(group, meta, keys, acc, dqs):
    return pl.pallas_call(
        enc_last_kernel,
        out_shape=[shaped((NB, OUT_ROWS, LANES), BF16), shaped(acc.shape, F32)],
        in_specs=[SMEM, SMEM] + [ANY] * 7,
        out_specs=[ANY, ANY],
        scratch_shapes=key_scratch() + score_scratch() + [
            pltpu.VMEM((LAST_TILES * TQ, LANES), F32),
            pltpu.VMEM((NQ_ENC + 8, LANES), F32),
            pltpu.VMEM((NB, OUT_ROWS, LANES), BF16),
            dma(ENC_TILES), dma(ENC_TILES), dma(ENC_TILES), dma(4), dma(4),
        ],
        input_output_aliases={6: 1},
        compiler_params=limit(38),
    )(group, meta, *keys, acc, *dqs)[0]


def dec_last(group, part, meta, keys, messages, back, enc_out):
    return pl.pallas_call(
        dec_last_kernel,
        out_shape=shaped((NB, OUT_ROWS, LANES), BF16),
        in_specs=[SMEM, SMEM, SMEM] + [ANY] * 10,
        out_specs=ANY,
        scratch_shapes=[pltpu.VMEM(k.shape, k.dtype) for k in keys] + [
            pltpu.VMEM((NK_DEC + TKD, LANES), F32),
            pltpu.VMEM((3, THERE_ROWS, LANES), BF16),
            pltpu.VMEM((3, BACK_ROWS, LANES), BF16),
            pltpu.VMEM((NK_DEC + TKD, LANES), F32),
            pltpu.VMEM((2 * TQ, LANES), F32),
            pltpu.VMEM((NB, OUT_ROWS, LANES), BF16),
            dma(3, 5), dma(),
        ],
        input_output_aliases={12: 0},
        compiler_params=limit(24),
    )(group, part, meta, *keys, *messages, *back, enc_out)


def on_device(queries, key_rows, value_rows, out_grad, enc_lengths, dec_lengths):
    group = lax.axis_index("grp").astype(jnp.int32).reshape(1)
    part = (lax.axis_index("blk") % 4).astype(jnp.int32).reshape(1)
    chunks = pl.pallas_call(
        pack_kernel,
        out_shape=shaped((NB, IN_ROWS, LANES), BF16),
        in_specs=[SMEM, SMEM, SMEM, SMEM, ANY, ANY, ANY, ANY],
        out_specs=ANY,
        scratch_shapes=[pltpu.VMEM((4, TOK, LANES), BF16)] * 4 + [pltpu.VMEM((8, TOK, LANES), F32)] * 2 + [
            pltpu.VMEM((NB, IN_ROWS, LANES), BF16), dma(4, 4), dma(4)],
        compiler_params=limit(62),
    )(group, part, enc_lengths, dec_lengths, queries, key_rows, value_rows, out_grad)
    held = lax.all_to_all(chunks, "blk", 0, 0, tiled=True)

    def partner(c, blk):
        return (blk + 16) % NB if c < 2 else blk

    there = [[(3 * NB + s, c * NB + partner(c, s)) for s in range(NB)] for c in range(3)]
    *dec_keys, m0, m1, m2, dec_meta = dec_first(group, part, held)
    messages = (m0, m1, m2)
    got = [lax.ppermute(messages[c], ("grp", "blk"), there[c]) for c in range(3)]
    *enc_keys, acc1, dq1, enc_meta = enc_first(group, held)
    acc2, dq2, answer = enc_dec(group, enc_meta, enc_keys, acc1, got)
    back = [lax.ppermute(answer, ("grp", "blk"), [(d, s) for s, d in there[c]]) for c in range(3)]
    enc_out = enc_last(group, enc_meta, enc_keys, acc2, (dq1, dq2))
    final = dec_last(group, part, dec_meta, dec_keys, messages, back, enc_out)
    final = lax.all_to_all(final, "blk", 0, 0, tiled=True)
    out = shaped(queries.shape, F32)
    return pl.pallas_call(
        unpack_kernel,
        out_shape=[out, out, out],
        in_specs=[SMEM, VMEM],
        out_specs=[VMEM, VMEM, VMEM],
        scratch_shapes=[pltpu.VMEM((TOK, LANES), F32)] * 3 + [pltpu.VMEM((DTOK, LANES), F32)],
        compiler_params=limit(10),
    )(group, final)


def solution(mesh):
    rows = P("blk", "grp")
    return jax.shard_map(
        on_device,
        mesh=mesh,
        in_specs=(rows, rows, rows, rows, P("blk"), P("blk")),
        out_specs=(rows, rows, rows),
        check_vma=False,
    )
```

profile of v0, /device:TPU:17, one launch (start us, length us, event | category | flops | bytes accessed | tf_op | source)
XLA Modules:
  0.0 105.7 jit_solution(9923446858401186998)
XLA Ops:
  1.9 2.8 %shard_map.85 = bf16[32,216,128]{2,1,0:T(8,128)(2,1)} custom-call(s32[1]{0:T(128)} %bitcast.group_ref, s32[1]{0:T(128)} %bitcast.1.part_ref, s32[1]{0:T(128)S(6)} %copy.15.enc_ref, s32[1]{0:T(128)S(6)} %copy.16.dec_ref, bf16[168,512]{1,0:T(8,128)(2,1)} %q_in.1, bf16[168,512]{1,0:T(8,128)(2,1)} %k_in.1, bf16[168,512]{1,0:T(8,128)(2,1)} %v_in.1, ...), custom_call_target="tpu_custom_call" | custom-call | tf_op jit(solution)/shard_map/pallas_call | solution.py:835
  4.7 32.2 %all_to_all.10.held_ref.y_ref = bf16[32,216,128]{2,1,0:T(8,128)(2,1)S(1)} all-to-all(bf16[32,216,128]{2,1,0:T(8,128)(2,1)} %shard_map.85), channel_id=1, replica_groups=mesh['grp'=4,'blk'=32] {'blk'}, dimensions={0} | all-to-all | bytes 3538944 | tf_op jit(solution)/shard_map/all_to_all | solution.py:844
  36.9 9.1 %shard_map.86 = (bf16[3,3072,128]{2,1,0:T(8,128)(2,1)S(1)}, bf16[3,3072,128]{2,1,0:T(8,128)(2,1)S(1)}, bf16[3,3,64,768]{3,2,1,0:T(8,128)(2,1)S(1)}, bf16[560,128...) custom-call(s32[1]{0:T(128)} %bitcast.group_ref, ...), custom_call_target="tpu_custom_call" | custom-call | tf_op jit(solution)/shard_map/pallas_call | solution.py:736
  46.1 1.3 %collective-permute-start = (bf16[560,128]{1,0:T(8,128)(2,1)S(1)}, bf16[560,128]{1,0:T(8,128)(2,1)S(1)}, u32[]{:S(2)}, u32[]{:S(2)}) collective-permute-start(bf16[560,128]{1,0:T(8,128)(2,1)S(1)} %get-tuple-element.25.m0_in), channel_id=1, source_target_pairs={{96,16},{97,17},{98,18},{99,19},{100,20},{101,21},{102,22},{103,23... | collective-permute-start | bytes 430088 | tf_op jit(solution)/shard_map/ppermute | solution.py:852
  47.4 1.3 %collective-permute-start.1 = (bf16[560,128]{1,0:T(8,128)(2,1)S(1)}, bf16[560,128]{1,0:T(8,128)(2,1)S(1)}, u32[]{:S(2)}, u32[]{:S(2)}) collective-permute-start(bf16[560,128]{1,0:T(8,128)(2,1)S(1)} %get-tuple-element.26.m1_in), channel_id=1, source_target_pairs={{96,48},{97,49},{98,50},{99,51},{100,52},{101,53},{102,54},{103,55... | collective-permute-start | bytes 430088 | tf_op jit(solution)/shard_map/ppermute | solution.py:852
  48.7 1.3 %collective-permute-start.2 = (bf16[560,128]{1,0:T(8,128)(2,1)S(1)}, bf16[560,128]{1,0:T(8,128)(2,1)S(1)}, u32[]{:S(2)}, u32[]{:S(2)}) collective-permute-start(bf16[560,128]{1,0:T(8,128)(2,1)S(1)} %get-tuple-element.27.m2_in), channel_id=1, source_target_pairs={{96,64},{97,65},{98,66},{99,67},{100,68},{101,69},{102,70},{103,71... | collective-permute-start | bytes 430088 | tf_op jit(solution)/shard_map/ppermute | solution.py:852
  50.0 0.7 shard_map.87
  50.7 0.0 collective-permute-done.m0_ref
  50.7 0.2 collective-permute-done.1.m1_ref
  50.9 0.0 collective-permute-done.2.m2_ref
  51.0 0.9 shard_map.88
  51.8 1.3 %collective-permute-start.5 = (bf16[544,128]{1,0:T(8,128)(2,1)S(1)}, bf16[544,128]{1,0:T(8,128)(2,1)S(1)}, u32[]{:S(2)}, u32[]{:S(2)}) collective-permute-start(bf16[544,128]{1,0:T(8,128)(2,1)S(1)} %get-tuple-element.34), channel_id=1, source_target_pairs={{64,96},{65,97},{66,98},{67,99},{68,100},{69,101},{70,102},{71,103... | collective-permute-start | bytes 417800 | tf_op jit(solution)/shard_map/ppermute | solution.py:855
  53.1 1.3 %collective-permute-start.4 = (bf16[544,128]{1,0:T(8,128)(2,1)S(1)}, bf16[544,128]{1,0:T(8,128)(2,1)S(1)}, u32[]{:S(2)}, u32[]{:S(2)}) collective-permute-start(bf16[544,128]{1,0:T(8,128)(2,1)S(1)} %get-tuple-element.34), channel_id=1, source_target_pairs={{48,96},{49,97},{50,98},{51,99},{52,100},{53,101},{54,102},{55,103... | collective-permute-start | bytes 417800 | tf_op jit(solution)/shard_map/ppermute | solution.py:855
  54.4 1.3 %collective-permute-start.3 = (bf16[544,128]{1,0:T(8,128)(2,1)S(1)}, bf16[544,128]{1,0:T(8,128)(2,1)S(1)}, u32[]{:S(2)}, u32[]{:S(2)}) collective-permute-start(bf16[544,128]{1,0:T(8,128)(2,1)S(1)} %get-tuple-element.34), channel_id=1, source_target_pairs={{16,96},{17,97},{18,98},{19,99},{20,100},{21,101},{22,102},{23,103... | collective-permute-start | bytes 417800 | tf_op jit(solution)/shard_map/ppermute | solution.py:855
  55.7 0.7 shard_map.89
  56.4 9.7 %collective-permute-done.5.b2_in = bf16[544,128]{1,0:T(8,128)(2,1)S(1)} collective-permute-done((bf16[544,128]{1,0:T(8,128)(2,1)S(1)}, bf16[544,128]{1,0:T(8,128)(2,1)S(1)}, u32[]{:S(2)}, u32[]{:S(2)}) %collective-permute-start.5) | collective-permute-done | bytes 139296 | tf_op jit(solution)/shard_map/ppermute | solution.py:855
  66.2 0.0 collective-permute-done.4.b1_in
  66.2 2.9 %collective-permute-done.3.b0_in = bf16[544,128]{1,0:T(8,128)(2,1)S(1)} collective-permute-done((bf16[544,128]{1,0:T(8,128)(2,1)S(1)}, bf16[544,128]{1,0:T(8,128)(2,1)S(1)}, u32[]{:S(2)}, u32[]{:S(2)}) %collective-permute-start.3) | collective-permute-done | bytes 139296 | tf_op jit(solution)/shard_map/ppermute | solution.py:855
  69.1 9.9 %shard_map.90 = bf16[32,192,128]{2,1,0:T(8,128)(2,1)S(1)} custom-call(s32[1]{0:T(128)} %bitcast.group_ref, s32[1]{0:T(128)} %bitcast.1.part_ref, s32[72]{0:T(128)S(1)} %get-tuple-element.21.meta_ref, bf16[3,3072,128]{2,1,0:T(8,128)(2,1)S(1)} %get-tuple-element.22.kv_in, ...), custom_call_target="tpu_custom_call", output_to_operand_aliasing={{}: (12, {})} | custom-call | tf_op jit(solution)/shard_map/pallas_call | solution.py:813
  78.9 25.4 %all_to_all.11.w_ref = bf16[32,192,128]{2,1,0:T(8,128)(2,1)S(1)} all-to-all(bf16[32,192,128]{2,1,0:T(8,128)(2,1)S(1)} %shard_map.90), channel_id=1, replica_groups=mesh['grp'=4,'blk'=32] {'blk'}, dimensions={0} | all-to-all | bytes 3145728 | tf_op jit(solution)/shard_map/all_to_all | solution.py:858
  104.3 1.4 %shard_map.91 = (f32[168,512]{1,0:T(8,128)}, f32[168,512]{1,0:T(8,128)}, f32[168,512]{1,0:T(8,128)}) custom-call(s32[1]{0:T(128)} %bitcast.group_ref, bf16[32,192,128]{2,1,0:T(8,128)(2,1)S(1)} %all_to_all.11.w_ref), custom_call_target="tpu_custom_call" | custom-call | tf_op jit(solution)/shard_map/pallas_call | solution.py:860
Async XLA Ops:
  46.1 4.6 %collective-permute-start = (bf16[560,128]{1,0:T(8,128)(2,1)S(1)}, bf16[560,128]{1,0:T(8,128)(2,1)S(1)}, u32[]{:S(2)}, u32[]{:S(2)}) collective-permute-start(bf16[560,128]{1,0:T(8,128)(2,1)S(1)} %get-tuple-element.25.m0_in), channel_id=1, source_target_pairs={{96,16},{97,17},{98,18},{99,19},{100,20},{101,21},{102,22},{103,23... | collective-permute-start | bytes 430088 | tf_op jit(solution)/shard_map/ppermute | solution.py:852
  47.4 3.6 %collective-permute-start.1 = (bf16[560,128]{1,0:T(8,128)(2,1)S(1)}, bf16[560,128]{1,0:T(8,128)(2,1)S(1)}, u32[]{:S(2)}, u32[]{:S(2)}) collective-permute-start(bf16[560,128]{1,0:T(8,128)(2,1)S(1)} %get-tuple-element.26.m1_in), channel_id=1, source_target_pairs={{96,48},{97,49},{98,50},{99,51},{100,52},{101,53},{102,54},{103,55... | collective-permute-start | bytes 430088 | tf_op jit(solution)/shard_map/ppermute | solution.py:852
  48.7 2.3 %collective-permute-start.2 = (bf16[560,128]{1,0:T(8,128)(2,1)S(1)}, bf16[560,128]{1,0:T(8,128)(2,1)S(1)}, u32[]{:S(2)}, u32[]{:S(2)}) collective-permute-start(bf16[560,128]{1,0:T(8,128)(2,1)S(1)} %get-tuple-element.27.m2_in), channel_id=1, source_target_pairs={{96,64},{97,65},{98,66},{99,67},{100,68},{101,69},{102,70},{103,71... | collective-permute-start | bytes 430088 | tf_op jit(solution)/shard_map/ppermute | solution.py:852
  51.8 14.3 %collective-permute-start.5 = (bf16[544,128]{1,0:T(8,128)(2,1)S(1)}, bf16[544,128]{1,0:T(8,128)(2,1)S(1)}, u32[]{:S(2)}, u32[]{:S(2)}) collective-permute-start(bf16[544,128]{1,0:T(8,128)(2,1)S(1)} %get-tuple-element.34), channel_id=1, source_target_pairs={{64,96},{65,97},{66,98},{67,99},{68,100},{69,101},{70,102},{71,103... | collective-permute-start | bytes 417800 | tf_op jit(solution)/shard_map/ppermute | solution.py:855
  53.1 13.0 %collective-permute-start.4 = (bf16[544,128]{1,0:T(8,128)(2,1)S(1)}, bf16[544,128]{1,0:T(8,128)(2,1)S(1)}, u32[]{:S(2)}, u32[]{:S(2)}) collective-permute-start(bf16[544,128]{1,0:T(8,128)(2,1)S(1)} %get-tuple-element.34), channel_id=1, source_target_pairs={{48,96},{49,97},{50,98},{51,99},{52,100},{53,101},{54,102},{55,103... | collective-permute-start | bytes 417800 | tf_op jit(solution)/shard_map/ppermute | solution.py:855
  54.4 14.6 %collective-permute-start.3 = (bf16[544,128]{1,0:T(8,128)(2,1)S(1)}, bf16[544,128]{1,0:T(8,128)(2,1)S(1)}, u32[]{:S(2)}, u32[]{:S(2)}) collective-permute-start(bf16[544,128]{1,0:T(8,128)(2,1)S(1)} %get-tuple-element.34), channel_id=1, source_target_pairs={{16,96},{17,97},{18,98},{19,99},{20,100},{21,101},{22,102},{23,103... | collective-permute-start | bytes 417800 | tf_op jit(solution)/shard_map/ppermute | solution.py:855
where the time goes:
time: 106 us
  blocking collectives  57.6 us (54%)
  Pallas kernels  25.4 us (24%)
  waiting for transfers between devices  12.9 us (12%)
  starting transfers between devices  7.77 us (7%)
  between operations  2.04 us (2%)
    all_to_all x1, blocking collectives, on_device(): held = lax.all_to_all(chunks, 'blk', 0, 0, tiled=True)  32.2 us
    all_to_all x1, blocking collectives, on_device(): final = lax.all_to_all(final, 'blk', 0, 0, tiled=True)  25.4 us
    ppermute x3, waiting for transfers between devices, on_device(): lax.ppermute(answer, ('grp', 'blk'), [(d, s) for s, d in there[c]])  12.6 us
    pallas_call x1, Pallas kernels, dec_last(): pl.pallas_call(dec_last_kernel, out_shape=shaped((NB, OUT_ROWS, LANES), B...  9.88 us
    pallas_call x1, Pallas kernels, dec_first(): pl.pallas_call(dec_first_kernel, out_shape=[shaped(*k) for k in keys] + [...  9.14 us
    ppermute x3, starting transfers between devices, on_device(): lax.ppermute(messages[c], ('grp', 'blk'), there[c])  3.9 us
    ppermute x3, starting transfers between devices, on_device(): lax.ppermute(answer, ('grp', 'blk'), [(d, s) for s, d in there[c]])  3.88 us
    pallas_call x1, Pallas kernels, on_device(): pl.pallas_call(pack_kernel, out_shape=shaped((NB, IN_ROWS, LANES), BF16),...  2.76 us
  transfers between devices with their start and end apart: 6, of which 3 were waited for; matrix products, arithmetic and copies ran while one was open for 0% of the time, Pallas kernels for 1%

commit v1 on v0

--- a/solution.py
+++ b/solution.py
@@ -27,7 +27,7 @@
 NK_ENC = -(-(NB * 176) // TK) * TK
 NK_DEC = -(-(NB * 64) // TKD) * TKD
 REST = 2 * TQ - DQ
-FIRST_TILES = 3
+FIRST_TILES = 2
 LAST_TILES = (NQ_ENC - REST) // TQ - FIRST_TILES
 THERE_ROWS = 2 * TQ + 48
 BACK_ROWS = 2 * TQ + 32
@@ -547,8 +547,8 @@
     ]
 
 
-def dec_first_kernel(group_ref, part_ref, held_ref, kv_out, ka_out, kt_out, m0_out, m1_out, m2_out, meta_ref,
-                     y_ref, kv_ref, ka_ref, kt_ref, pos_ref, m_ref, qg_s, stat_s, sems, wide_s, lens_s, sem):
+def dec_first_kernel(group_ref, part_ref, held_ref, kv_out, ka_out, m0_out, m1_out, m2_out, meta_ref,
+                     y_ref, kv_ref, ka_ref, pos_ref, m_ref, qg_s, stat_s, sems, wide_s, lens_s, sem):
     @pl.when(group_ref[0] == 3)
     def _():
         fetch = pltpu.make_async_copy(held_ref, y_ref, sems.at[0])
@@ -556,40 +556,31 @@
         fetch.wait()
         read_lens(y_ref, wide_s, lens_s, sem)
 
-        def block(b, offset):
+        end = jnp.int32(0)
+        for b in range(NB):
             length = lens_s[7, b]
-            meta_ref[b] = offset
+            meta_ref[b] = end
             meta_ref[NB + b] = length
             chunk = y_ref[b].astype(F32)
             for c in range(3):
                 keys = chunk[DIN_ROWS * c : DIN_ROWS * c + 64].astype(BF16)
-                place_block(kv_ref.at[c], ka_ref.at[c], keys, offset, length)
-            put_pos(pos_ref, offset, b)
-            return offset + ((length + 15) // 16) * 16
-
-        end = lax.fori_loop(0, NB, block, jnp.int32(0))
+                place_block(kv_ref.at[c], ka_ref.at[c], keys, end, length)
+                qg_s[c, pl.ds(DQTR * b, 16), :] = chunk[DIN_ROWS * c + DTOK : DIN_ROWS * (c + 1)]
+            put_pos(pos_ref, end, b)
+            end = end + ((length + 15) // 16) * 16
         for c in range(3):
             place_padding(kv_ref.at[c], ka_ref.at[c], end, TKD)
         tiles = (end + TKD - 1) // TKD
         meta_ref[2 * NB] = tiles
-        for b in range(NB):
-            chunk = y_ref[b].astype(F32)
-            for c in range(3):
-                qg_s[c, pl.ds(DQTR * b, 16), :] = chunk[DIN_ROWS * c + DTOK : DIN_ROWS * (c + 1)]
         part = part_ref[0]
         stat_s[...] = jnp.zeros_like(stat_s)
         for c in range(3):
             qg_s[c, pl.ds(DQ, REST), :] = jnp.zeros((REST, LANES), F32)
             m_ref[c, pl.ds(0, 2 * TQ), :] = qg_s[c].astype(BF16)
 
-            @pl.loop(0, tiles)
-            def _(kt):
-                kt_ref[c, kt] = turn(kv_ref[c, tile_rows(kt, TKD), :])
-
         copies = [
             pltpu.make_async_copy(src, dst, sems.at[1 + i])
-            for i, (src, dst) in enumerate(
-                ((kv_ref, kv_out), (ka_ref, ka_out), (kt_ref, kt_out)))
+            for i, (src, dst) in enumerate(((kv_ref, kv_out), (ka_ref, ka_out)))
         ]
         for copy in copies:
             copy.start()
@@ -620,8 +611,8 @@
             copy.wait()
 
 
-def dec_last_kernel(group_ref, part_ref, meta_ref, kv_in, ka_in, kt_in, m0_in, m1_in, m2_in, b0_in, b1_in, b2_in, enc_ref,
-                    o_ref, kv_ref, ka_ref, kt_ref, pos_ref, m_ref, back_ref, acc_s, dq_s, out_s, sems, sem):
+def dec_last_kernel(group_ref, part_ref, meta_ref, kv_ref, ka_ref, m0_in, m1_in, m2_in, b0_in, b1_in, b2_in, enc_ref,
+                    o_ref, pos_ref, m_ref, back_ref, acc_s, dq_s, out_s, sems, out_sem):
     @pl.when(group_ref[0] == 3)
     def _():
         tiles = meta_ref[2 * NB]
@@ -629,8 +620,7 @@
         fetches = [
             [
                 pltpu.make_async_copy(src, dst.at[c], sems.at[c, i])
-                for i, (src, dst) in enumerate(
-                    ((m_in, m_ref), (b_in, back_ref), (kv_in.at[c], kv_ref), (ka_in.at[c], ka_ref), (kt_in.at[c], kt_ref)))
+                for i, (src, dst) in enumerate(((m_in, m_ref), (b_in, back_ref)))
             ]
             for c, (m_in, b_in) in enumerate(((m0_in, b0_in), (m1_in, b1_in), (m2_in, b2_in)))
         ]
@@ -665,7 +655,8 @@
                     parts = grad_parts(*found, total[t], delta[t])
                     grad = key_grads(parts, naturals[t])
                     acc_s[rows, :] = grad if t == 0 else acc_s[rows, :] + grad
-                    keys = kt_ref[c, kt, :, u // 2 * SUB : (u // 2 + 1) * SUB]
+                    if t == 0:
+                        keys = turn(kv_ref[c, rows, :])
                     dqs[t] = dqs[t] + jnp.dot(keys, parts[1], preferred_element_type=F32)
                     found = fresh
                 return tuple(dqs)
@@ -683,9 +674,12 @@
                 base = DQTR * b
                 dq = jnp.where(lane_low((8, LANES)), dq_s[pl.ds(base, 8), :], dq_s[pl.ds(base + 7, 8), :])
                 out_s[b, pl.ds(DOUT_ROWS * c, DOUT_ROWS), :] = jnp.concatenate([grad, dq], axis=0).astype(BF16)
-        copy = pltpu.make_async_copy(out_s, o_ref, sem)
-        copy.start()
-        copy.wait()
+                if c == 2 and b % 8 == 7:
+                    some = pl.ds(b - 7, 8)
+                    pltpu.make_async_copy(out_s.at[some], o_ref.at[some], out_sem.at[b // 8]).start()
+        for i in range(NB // 8):
+            some = pl.ds(8 * i, 8)
+            pltpu.make_async_copy(out_s.at[some], o_ref.at[some], out_sem.at[i]).wait()
 
 
 SMEM = pl.BlockSpec(memory_space=pltpu.SMEM)
@@ -730,14 +724,13 @@
 
 
 def dec_first(group, part, held):
-    keys = [((3, NK_DEC + TKD, LANES), BF16), ((3, NK_DEC + TKD, LANES), BF16),
-            ((3, NK_DEC // TKD, HD, TKD), BF16)]
+    keys = [((3, NK_DEC + TKD, LANES), BF16), ((3, NK_DEC + TKD, LANES), BF16)]
     pos = ((NK_DEC + TKD, LANES), F32)
     return pl.pallas_call(
         dec_first_kernel,
         out_shape=[shaped(*k) for k in keys] + [shaped((THERE_ROWS, LANES), BF16)] * 3 + [META],
         in_specs=[SMEM, SMEM, ANY],
-        out_specs=[ANY] * 6 + [SMEM],
+        out_specs=[ANY] * 5 + [SMEM],
         scratch_shapes=[pltpu.VMEM(held.shape, BF16)] + [pltpu.VMEM(*k) for k in keys + [pos]] + [
             pltpu.VMEM((3, THERE_ROWS, LANES), BF16),
             pltpu.VMEM((3, 2 * TQ, LANES), F32),
@@ -813,18 +806,18 @@
     return pl.pallas_call(
         dec_last_kernel,
         out_shape=shaped((NB, OUT_ROWS, LANES), BF16),
-        in_specs=[SMEM, SMEM, SMEM] + [ANY] * 10,
+        in_specs=[SMEM, SMEM, SMEM] + [VMEM] * 2 + [ANY] * 7,
         out_specs=ANY,
-        scratch_shapes=[pltpu.VMEM(k.shape, k.dtype) for k in keys] + [
+        scratch_shapes=[
             pltpu.VMEM((NK_DEC + TKD, LANES), F32),
             pltpu.VMEM((3, THERE_ROWS, LANES), BF16),
             pltpu.VMEM((3, BACK_ROWS, LANES), BF16),
             pltpu.VMEM((NK_DEC + TKD, LANES), F32),
             pltpu.VMEM((2 * TQ, LANES), F32),
             pltpu.VMEM((NB, OUT_ROWS, LANES), BF16),
-            dma(3, 5), dma(),
+            dma(3, 2), dma(4),
         ],
-        input_output_aliases={12: 0},
+        input_output_aliases={11: 0},
         compiler_params=limit(24),
     )(group, part, meta, *keys, *messages, *back, enc_out)
 
@@ -852,7 +845,7 @@
     got = [lax.ppermute(messages[c], ("grp", "blk"), there[c]) for c in range(3)]
     *enc_keys, acc1, dq1, enc_meta = enc_first(group, held)
     acc2, dq2, answer = enc_dec(group, enc_meta, enc_keys, acc1, got)
-    back = [lax.ppermute(answer, ("grp", "blk"), [(d, s) for s, d in there[c]]) for c in range(3)]
+    back = [lax.ppermute(answer, ("grp", "blk"), [(d, s) for s, d in there[c]]) for c in (2, 1, 0)][::-1]
     enc_out = enc_last(group, enc_meta, enc_keys, acc2, (dq1, dq2))
     final = dec_last(group, part, dec_meta, dec_keys, messages, back, enc_out)
     final = lax.all_to_all(final, "blk", 0, 0, tiled=True)

time: 106 us -> 106 us (level)
  blocking collectives: 57.6 us -> 60.1 us
  waiting for transfers between devices: 12.9 us -> 10.8 us
    all_to_all x1, blocking collectives: 25.4 us -> 27.9 us  [on_device(): final = lax.all_to_all(final, 'blk', 0, 0, tiled=True)]
    ppermute x3, waiting for transfers between devices: 12.6 us -> 10.5 us  [on_device(): lax.ppermute(answer, ('grp', 'blk'), [(d, s) for s, d in there[c]])]
    pallas_call x1, Pallas kernels: 9.14 us -> 8.01 us  [dec_first(): pl.pallas_call(dec_first_kernel, out_shape=[shaped(*k) for k in keys] + [...]
  transfers between devices with their start and end apart: 6 -> 6, of which waited for: 3 -> 4; matrix products, arithmetic and copies ran while one was open for 0% -> 0% of each run, Pallas kernels for 1% -> 1%
where the time goes in v1:
time: 106 us; the launch traced here: 105 us
  blocking collectives  60.1 us (57%)
  Pallas kernels  24.4 us (23%)
  waiting for transfers between devices  10.8 us (10%)
  starting transfers between devices  7.77 us (7%)
  between operations  2.04 us (2%)
    all_to_all x1, blocking collectives, on_device(): held = lax.all_to_all(chunks, 'blk', 0, 0, tiled=True)  32.2 us
    all_to_all x1, blocking collectives, on_device(): final = lax.all_to_all(final, 'blk', 0, 0, tiled=True)  27.9 us
    ppermute x3, waiting for transfers between devices, on_device(): lax.ppermute(answer, ('grp', 'blk'), [(d, s) for s, d in there[c]])  10.5 us
    pallas_call x1, Pallas kernels, dec_last(): pl.pallas_call(dec_last_kernel, out_shape=shaped((NB, OUT_ROWS, LANES), B...  10 us
    pallas_call x1, Pallas kernels, dec_first(): pl.pallas_call(dec_first_kernel, out_shape=[shaped(*k) for k in keys] + [...  8.01 us
    ppermute x3, starting transfers between devices, on_device(): lax.ppermute(messages[c], ('grp', 'blk'), there[c])  3.9 us
    ppermute x3, starting transfers between devices, on_device(): lax.ppermute(answer, ('grp', 'blk'), [(d, s) for s, d in there[c]])  3.88 us
    pallas_call x1, Pallas kernels, on_device(): pl.pallas_call(pack_kernel, out_shape=shaped((NB, IN_ROWS, LANES), BF16),...  2.76 us
  transfers between devices with their start and end apart: 6, of which 4 were waited for; matrix products, arithmetic and copies ran while one was open for 0% of the time, Pallas kernels for 1%

profile of v1, /device:TPU:17, one launch (start us, length us, event | category | flops | bytes accessed | tf_op | source)
XLA Modules:
  0.0 105.1 jit_solution(8083329207702841919)
XLA Ops:
  1.9 2.8 %shard_map.85 = bf16[32,216,128]{2,1,0:T(8,128)(2,1)} custom-call(s32[1]{0:T(128)} %bitcast.group_ref, s32[1]{0:T(128)} %bitcast.1.part_ref, s32[1]{0:T(128)S(6)} %copy.15.enc_ref, s32[1]{0:T(128)S(6)} %copy.16.dec_ref, bf16[168,512]{1,0:T(8,128)(2,1)} %q_in.1, bf16[168,512]{1,0:T(8,128)(2,1)} %k_in.1, bf16[168,512]{1,0:T(8,128)(2,1)} %v_in.1, ...), custom_call_target="tpu_custom_call" | custom-call | tf_op jit(solution)/shard_map/pallas_call | solution.py:828
  4.7 32.2 %all_to_all.10.held_ref.y_ref = bf16[32,216,128]{2,1,0:T(8,128)(2,1)S(1)} all-to-all(bf16[32,216,128]{2,1,0:T(8,128)(2,1)} %shard_map.85), channel_id=1, replica_groups=mesh['grp'=4,'blk'=32] {'blk'}, dimensions={0} | all-to-all | bytes 3538944 | tf_op jit(solution)/shard_map/all_to_all | solution.py:837
  36.9 8.0 %shard_map.86 = (bf16[3,3072,128]{2,1,0:T(8,128)(2,1)S(1)}, bf16[3,3072,128]{2,1,0:T(8,128)(2,1)S(1)}, bf16[560,128]{1,0:T(8,128)(2,1)S(1)}, bf16[560,128]{1,0:T...) custom-call(s32[1]{0:T(128)} %bitcast.group_ref, s32[1]{0:T(128)} %bitcast.1.part_ref, ...), custom_call_target="tpu_custom_call" | custom-call | tf_op jit(solution)/shard_map/pallas_call | solution.py:729
  44.9 1.3 %collective-permute-start = (bf16[560,128]{1,0:T(8,128)(2,1)S(1)}, bf16[560,128]{1,0:T(8,128)(2,1)S(1)}, u32[]{:S(2)}, u32[]{:S(2)}) collective-permute-start(bf16[560,128]{1,0:T(8,128)(2,1)S(1)} %get-tuple-element.23.m0_in), channel_id=1, source_target_pairs={{96,16},{97,17},{98,18},{99,19},{100,20},{101,21},{102,22},{103,23... | collective-permute-start | bytes 430088 | tf_op jit(solution)/shard_map/ppermute | solution.py:845
  46.2 1.3 %collective-permute-start.1 = (bf16[560,128]{1,0:T(8,128)(2,1)S(1)}, bf16[560,128]{1,0:T(8,128)(2,1)S(1)}, u32[]{:S(2)}, u32[]{:S(2)}) collective-permute-start(bf16[560,128]{1,0:T(8,128)(2,1)S(1)} %get-tuple-element.24.m1_in), channel_id=1, source_target_pairs={{96,48},{97,49},{98,50},{99,51},{100,52},{101,53},{102,54},{103,55... | collective-permute-start | bytes 430088 | tf_op jit(solution)/shard_map/ppermute | solution.py:845
  47.5 1.3 %collective-permute-start.2 = (bf16[560,128]{1,0:T(8,128)(2,1)S(1)}, bf16[560,128]{1,0:T(8,128)(2,1)S(1)}, u32[]{:S(2)}, u32[]{:S(2)}) collective-permute-start(bf16[560,128]{1,0:T(8,128)(2,1)S(1)} %get-tuple-element.25.m2_in), channel_id=1, source_target_pairs={{96,64},{97,65},{98,66},{99,67},{100,68},{101,69},{102,70},{103,71... | collective-permute-start | bytes 430088 | tf_op jit(solution)/shard_map/ppermute | solution.py:845
  48.8 0.7 shard_map.87
  49.5 0.0 collective-permute-done.m0_ref
  49.6 0.2 collective-permute-done.1.m1_ref
  49.8 0.0 collective-permute-done.2.m2_ref
  49.8 0.9 shard_map.88
  50.7 1.3 %collective-permute-start.5 = (bf16[544,128]{1,0:T(8,128)(2,1)S(1)}, bf16[544,128]{1,0:T(8,128)(2,1)S(1)}, u32[]{:S(2)}, u32[]{:S(2)}) collective-permute-start(bf16[544,128]{1,0:T(8,128)(2,1)S(1)} %get-tuple-element.32), channel_id=1, source_target_pairs={{64,96},{65,97},{66,98},{67,99},{68,100},{69,101},{70,102},{71,103... | collective-permute-start | bytes 417800 | tf_op jit(solution)/shard_map/ppermute | solution.py:848
  52.0 1.3 %collective-permute-start.4 = (bf16[544,128]{1,0:T(8,128)(2,1)S(1)}, bf16[544,128]{1,0:T(8,128)(2,1)S(1)}, u32[]{:S(2)}, u32[]{:S(2)}) collective-permute-start(bf16[544,128]{1,0:T(8,128)(2,1)S(1)} %get-tuple-element.32), channel_id=1, source_target_pairs={{48,96},{49,97},{50,98},{51,99},{52,100},{53,101},{54,102},{55,103... | collective-permute-start | bytes 417800 | tf_op jit(solution)/shard_map/ppermute | solution.py:848
  53.3 1.3 %collective-permute-start.3 = (bf16[544,128]{1,0:T(8,128)(2,1)S(1)}, bf16[544,128]{1,0:T(8,128)(2,1)S(1)}, u32[]{:S(2)}, u32[]{:S(2)}) collective-permute-start(bf16[544,128]{1,0:T(8,128)(2,1)S(1)} %get-tuple-element.32), channel_id=1, source_target_pairs={{16,96},{17,97},{18,98},{19,99},{20,100},{21,101},{22,102},{23,103... | collective-permute-start | bytes 417800 | tf_op jit(solution)/shard_map/ppermute | solution.py:848
  54.6 0.7 shard_map.89
  55.3 7.4 %collective-permute-done.5.b2_in = bf16[544,128]{1,0:T(8,128)(2,1)S(1)} collective-permute-done((bf16[544,128]{1,0:T(8,128)(2,1)S(1)}, bf16[544,128]{1,0:T(8,128)(2,1)S(1)}, u32[]{:S(2)}, u32[]{:S(2)}) %collective-permute-start.5) | collective-permute-done | bytes 139296 | tf_op jit(solution)/shard_map/ppermute | solution.py:848
  62.7 1.7 %collective-permute-done.4.b1_in = bf16[544,128]{1,0:T(8,128)(2,1)S(1)} collective-permute-done((bf16[544,128]{1,0:T(8,128)(2,1)S(1)}, bf16[544,128]{1,0:T(8,128)(2,1)S(1)}, u32[]{:S(2)}, u32[]{:S(2)}) %collective-permute-start.4) | collective-permute-done | bytes 139296 | tf_op jit(solution)/shard_map/ppermute | solution.py:848
  64.5 1.3 %collective-permute-done.3.b0_in = bf16[544,128]{1,0:T(8,128)(2,1)S(1)} collective-permute-done((bf16[544,128]{1,0:T(8,128)(2,1)S(1)}, bf16[544,128]{1,0:T(8,128)(2,1)S(1)}, u32[]{:S(2)}, u32[]{:S(2)}) %collective-permute-start.3) | collective-permute-done | bytes 139296 | tf_op jit(solution)/shard_map/ppermute | solution.py:848
  65.8 10.0 %shard_map.90 = bf16[32,192,128]{2,1,0:T(8,128)(2,1)S(1)} custom-call(s32[1]{0:T(128)} %bitcast.group_ref, s32[1]{0:T(128)} %bitcast.1.part_ref, s32[72]{0:T(128)S(1)} %get-tuple-element.20.meta_ref, bf16[3,3072,128]{2,1,0:T(8,128)(2,1)S(1)} %get-tuple-element.21.kv_ref, ...), custom_call_target="tpu_custom_call", output_to_operand_aliasing={{}: (11, {})} | custom-call | tf_op jit(solution)/shard_map/pallas_call | solution.py:806
  75.9 27.9 %all_to_all.11.w_ref = bf16[32,192,128]{2,1,0:T(8,128)(2,1)S(1)} all-to-all(bf16[32,192,128]{2,1,0:T(8,128)(2,1)S(1)} %shard_map.90), channel_id=1, replica_groups=mesh['grp'=4,'blk'=32] {'blk'}, dimensions={0} | all-to-all | bytes 3145728 | tf_op jit(solution)/shard_map/all_to_all | solution.py:851
  103.8 1.4 %shard_map.91 = (f32[168,512]{1,0:T(8,128)}, f32[168,512]{1,0:T(8,128)}, f32[168,512]{1,0:T(8,128)}) custom-call(s32[1]{0:T(128)} %bitcast.group_ref, bf16[32,192,128]{2,1,0:T(8,128)(2,1)S(1)} %all_to_all.11.w_ref), custom_call_target="tpu_custom_call" | custom-call | tf_op jit(solution)/shard_map/pallas_call | solution.py:853
Async XLA Ops:
  44.9 4.6 %collective-permute-start = (bf16[560,128]{1,0:T(8,128)(2,1)S(1)}, bf16[560,128]{1,0:T(8,128)(2,1)S(1)}, u32[]{:S(2)}, u32[]{:S(2)}) collective-permute-start(bf16[560,128]{1,0:T(8,128)(2,1)S(1)} %get-tuple-element.23.m0_in), channel_id=1, source_target_pairs={{96,16},{97,17},{98,18},{99,19},{100,20},{101,21},{102,22},{103,23... | collective-permute-start | bytes 430088 | tf_op jit(solution)/shard_map/ppermute | solution.py:845
  46.2 3.6 %collective-permute-start.1 = (bf16[560,128]{1,0:T(8,128)(2,1)S(1)}, bf16[560,128]{1,0:T(8,128)(2,1)S(1)}, u32[]{:S(2)}, u32[]{:S(2)}) collective-permute-start(bf16[560,128]{1,0:T(8,128)(2,1)S(1)} %get-tuple-element.24.m1_in), channel_id=1, source_target_pairs={{96,48},{97,49},{98,50},{99,51},{100,52},{101,53},{102,54},{103,55... | collective-permute-start | bytes 430088 | tf_op jit(solution)/shard_map/ppermute | solution.py:845
  47.5 2.3 %collective-permute-start.2 = (bf16[560,128]{1,0:T(8,128)(2,1)S(1)}, bf16[560,128]{1,0:T(8,128)(2,1)S(1)}, u32[]{:S(2)}, u32[]{:S(2)}) collective-permute-start(bf16[560,128]{1,0:T(8,128)(2,1)S(1)} %get-tuple-element.25.m2_in), channel_id=1, source_target_pairs={{96,64},{97,65},{98,66},{99,67},{100,68},{101,69},{102,70},{103,71... | collective-permute-start | bytes 430088 | tf_op jit(solution)/shard_map/ppermute | solution.py:845
  50.7 12.0 %collective-permute-start.5 = (bf16[544,128]{1,0:T(8,128)(2,1)S(1)}, bf16[544,128]{1,0:T(8,128)(2,1)S(1)}, u32[]{:S(2)}, u32[]{:S(2)}) collective-permute-start(bf16[544,128]{1,0:T(8,128)(2,1)S(1)} %get-tuple-element.32), channel_id=1, source_target_pairs={{64,96},{65,97},{66,98},{67,99},{68,100},{69,101},{70,102},{71,103... | collective-permute-start | bytes 417800 | tf_op jit(solution)/shard_map/ppermute | solution.py:848
  52.0 12.5 %collective-permute-start.4 = (bf16[544,128]{1,0:T(8,128)(2,1)S(1)}, bf16[544,128]{1,0:T(8,128)(2,1)S(1)}, u32[]{:S(2)}, u32[]{:S(2)}) collective-permute-start(bf16[544,128]{1,0:T(8,128)(2,1)S(1)} %get-tuple-element.32), channel_id=1, source_target_pairs={{48,96},{49,97},{50,98},{51,99},{52,100},{53,101},{54,102},{55,103... | collective-permute-start | bytes 417800 | tf_op jit(solution)/shard_map/ppermute | solution.py:848
  53.3 12.5 %collective-permute-start.3 = (bf16[544,128]{1,0:T(8,128)(2,1)S(1)}, bf16[544,128]{1,0:T(8,128)(2,1)S(1)}, u32[]{:S(2)}, u32[]{:S(2)}) collective-permute-start(bf16[544,128]{1,0:T(8,128)(2,1)S(1)} %get-tuple-element.32), channel_id=1, source_target_pairs={{16,96},{17,97},{18,98},{19,99},{20,100},{21,101},{22,102},{23,103... | collective-permute-start | bytes 417800 | tf_op jit(solution)/shard_map/ppermute | solution.py:848

commit v2 on v1

--- a/solution.py
+++ b/solution.py
@@ -27,7 +27,7 @@
 NK_ENC = -(-(NB * 176) // TK) * TK
 NK_DEC = -(-(NB * 64) // TKD) * TKD
 REST = 2 * TQ - DQ
-FIRST_TILES = 2
+FIRST_TILES = 3
 LAST_TILES = (NQ_ENC - REST) // TQ - FIRST_TILES
 THERE_ROWS = 2 * TQ + 48
 BACK_ROWS = 2 * TQ + 32

time: 106 us -> 106 us (level)
  waiting for transfers between devices: 10.8 us -> 14 us
  blocking collectives: 60.1 us -> 57.4 us
    ppermute x3, waiting for transfers between devices: 10.5 us -> 13.8 us  [on_device(): lax.ppermute(answer, ('grp', 'blk'), [(d, s) for s, d in there[c]])]
    all_to_all x1, blocking collectives: 27.9 us -> 25.2 us  [on_device(): final = lax.all_to_all(final, 'blk', 0, 0, tiled=True)]
  transfers between devices with their start and end apart: 6 -> 6, of which waited for: 4 -> 3; matrix products, arithmetic and copies ran while one was open for 0% -> 0% of each run, Pallas kernels for 1% -> 1%
where the time goes in v2:
time: 106 us
  blocking collectives  57.4 us (54%)
  Pallas kernels  24.4 us (23%)
  waiting for transfers between devices  14 us (13%)
  starting transfers between devices  7.77 us (7%)
  between operations  2.04 us (2%)
    all_to_all x1, blocking collectives, on_device(): held = lax.all_to_all(chunks, 'blk', 0, 0, tiled=True)  32.2 us
    all_to_all x1, blocking collectives, on_device(): final = lax.all_to_all(final, 'blk', 0, 0, tiled=True)  25.2 us
    ppermute x3, waiting for transfers between devices, on_device(): lax.ppermute(answer, ('grp', 'blk'), [(d, s) for s, d in there[c]])  13.8 us
    pallas_call x1, Pallas kernels, dec_last(): pl.pallas_call(dec_last_kernel, out_shape=shaped((NB, OUT_ROWS, LANES), B...  10 us
    pallas_call x1, Pallas kernels, dec_first(): pl.pallas_call(dec_first_kernel, out_shape=[shaped(*k) for k in keys] + [...  8.01 us
    ppermute x3, starting transfers between devices, on_device(): lax.ppermute(messages[c], ('grp', 'blk'), there[c])  3.9 us
    ppermute x3, starting transfers between devices, on_device(): lax.ppermute(answer, ('grp', 'blk'), [(d, s) for s, d in there[c]])  3.88 us
    pallas_call x1, Pallas kernels, on_device(): pl.pallas_call(pack_kernel, out_shape=shaped((NB, IN_ROWS, LANES), BF16),...  2.76 us
  transfers between devices with their start and end apart: 6, of which 3 were waited for; matrix products, arithmetic and copies ran while one was open for 0% of the time, Pallas kernels for 1%

profile of v2, /device:TPU:17, one launch (start us, length us, event | category | flops | bytes accessed | tf_op | source)
XLA Modules:
  0.0 105.6 jit_solution(15194361801282342460)
XLA Ops:
  1.9 2.8 %shard_map.85 = bf16[32,216,128]{2,1,0:T(8,128)(2,1)} custom-call(s32[1]{0:T(128)} %bitcast.group_ref, s32[1]{0:T(128)} %bitcast.1.part_ref, s32[1]{0:T(128)S(6)} %copy.15.enc_ref, s32[1]{0:T(128)S(6)} %copy.16.dec_ref, bf16[168,512]{1,0:T(8,128)(2,1)} %q_in.1, bf16[168,512]{1,0:T(8,128)(2,1)} %k_in.1, bf16[168,512]{1,0:T(8,128)(2,1)} %v_in.1, ...), custom_call_target="tpu_custom_call" | custom-call | tf_op jit(solution)/shard_map/pallas_call | solution.py:828
  4.7 32.2 %all_to_all.10.held_ref.y_ref = bf16[32,216,128]{2,1,0:T(8,128)(2,1)S(1)} all-to-all(bf16[32,216,128]{2,1,0:T(8,128)(2,1)} %shard_map.85), channel_id=1, replica_groups=mesh['grp'=4,'blk'=32] {'blk'}, dimensions={0} | all-to-all | bytes 3538944 | tf_op jit(solution)/shard_map/all_to_all | solution.py:837
  36.9 8.0 %shard_map.86 = (bf16[3,3072,128]{2,1,0:T(8,128)(2,1)S(1)}, bf16[3,3072,128]{2,1,0:T(8,128)(2,1)S(1)}, bf16[560,128]{1,0:T(8,128)(2,1)S(1)}, bf16[560,128]{1,0:T...) custom-call(s32[1]{0:T(128)} %bitcast.group_ref, s32[1]{0:T(128)} %bitcast.1.part_ref, ...), custom_call_target="tpu_custom_call" | custom-call | tf_op jit(solution)/shard_map/pallas_call | solution.py:729
  44.9 1.3 %collective-permute-start = (bf16[560,128]{1,0:T(8,128)(2,1)S(1)}, bf16[560,128]{1,0:T(8,128)(2,1)S(1)}, u32[]{:S(2)}, u32[]{:S(2)}) collective-permute-start(bf16[560,128]{1,0:T(8,128)(2,1)S(1)} %get-tuple-element.23.m0_in), channel_id=1, source_target_pairs={{96,16},{97,17},{98,18},{99,19},{100,20},{101,21},{102,22},{103,23... | collective-permute-start | bytes 430088 | tf_op jit(solution)/shard_map/ppermute | solution.py:845
  46.2 1.3 %collective-permute-start.1 = (bf16[560,128]{1,0:T(8,128)(2,1)S(1)}, bf16[560,128]{1,0:T(8,128)(2,1)S(1)}, u32[]{:S(2)}, u32[]{:S(2)}) collective-permute-start(bf16[560,128]{1,0:T(8,128)(2,1)S(1)} %get-tuple-element.24.m1_in), channel_id=1, source_target_pairs={{96,48},{97,49},{98,50},{99,51},{100,52},{101,53},{102,54},{103,55... | collective-permute-start | bytes 430088 | tf_op jit(solution)/shard_map/ppermute | solution.py:845
  47.5 1.3 %collective-permute-start.2 = (bf16[560,128]{1,0:T(8,128)(2,1)S(1)}, bf16[560,128]{1,0:T(8,128)(2,1)S(1)}, u32[]{:S(2)}, u32[]{:S(2)}) collective-permute-start(bf16[560,128]{1,0:T(8,128)(2,1)S(1)} %get-tuple-element.25.m2_in), channel_id=1, source_target_pairs={{96,64},{97,65},{98,66},{99,67},{100,68},{101,69},{102,70},{103,71... | collective-permute-start | bytes 430088 | tf_op jit(solution)/shard_map/ppermute | solution.py:845
  48.8 0.7 shard_map.87
  49.5 0.0 collective-permute-done.m0_ref
  49.6 0.2 collective-permute-done.1.m1_ref
  49.8 0.0 collective-permute-done.2.m2_ref
  49.8 0.9 shard_map.88
  50.7 1.3 %collective-permute-start.5 = (bf16[544,128]{1,0:T(8,128)(2,1)S(1)}, bf16[544,128]{1,0:T(8,128)(2,1)S(1)}, u32[]{:S(2)}, u32[]{:S(2)}) collective-permute-start(bf16[544,128]{1,0:T(8,128)(2,1)S(1)} %get-tuple-element.32), channel_id=1, source_target_pairs={{64,96},{65,97},{66,98},{67,99},{68,100},{69,101},{70,102},{71,103... | collective-permute-start | bytes 417800 | tf_op jit(solution)/shard_map/ppermute | solution.py:848
  52.0 1.3 %collective-permute-start.4 = (bf16[544,128]{1,0:T(8,128)(2,1)S(1)}, bf16[544,128]{1,0:T(8,128)(2,1)S(1)}, u32[]{:S(2)}, u32[]{:S(2)}) collective-permute-start(bf16[544,128]{1,0:T(8,128)(2,1)S(1)} %get-tuple-element.32), channel_id=1, source_target_pairs={{48,96},{49,97},{50,98},{51,99},{52,100},{53,101},{54,102},{55,103... | collective-permute-start | bytes 417800 | tf_op jit(solution)/shard_map/ppermute | solution.py:848
  53.3 1.3 %collective-permute-start.3 = (bf16[544,128]{1,0:T(8,128)(2,1)S(1)}, bf16[544,128]{1,0:T(8,128)(2,1)S(1)}, u32[]{:S(2)}, u32[]{:S(2)}) collective-permute-start(bf16[544,128]{1,0:T(8,128)(2,1)S(1)} %get-tuple-element.32), channel_id=1, source_target_pairs={{16,96},{17,97},{18,98},{19,99},{20,100},{21,101},{22,102},{23,103... | collective-permute-start | bytes 417800 | tf_op jit(solution)/shard_map/ppermute | solution.py:848
  54.6 0.7 shard_map.89
  55.3 10.9 %collective-permute-done.5.b2_in = bf16[544,128]{1,0:T(8,128)(2,1)S(1)} collective-permute-done((bf16[544,128]{1,0:T(8,128)(2,1)S(1)}, bf16[544,128]{1,0:T(8,128)(2,1)S(1)}, u32[]{:S(2)}, u32[]{:S(2)}) %collective-permute-start.5) | collective-permute-done | bytes 139296 | tf_op jit(solution)/shard_map/ppermute | solution.py:848
  66.2 0.0 collective-permute-done.4.b1_in
  66.2 2.9 %collective-permute-done.3.b0_in = bf16[544,128]{1,0:T(8,128)(2,1)S(1)} collective-permute-done((bf16[544,128]{1,0:T(8,128)(2,1)S(1)}, bf16[544,128]{1,0:T(8,128)(2,1)S(1)}, u32[]{:S(2)}, u32[]{:S(2)}) %collective-permute-start.3) | collective-permute-done | bytes 139296 | tf_op jit(solution)/shard_map/ppermute | solution.py:848
  69.1 10.0 %shard_map.90 = bf16[32,192,128]{2,1,0:T(8,128)(2,1)S(1)} custom-call(s32[1]{0:T(128)} %bitcast.group_ref, s32[1]{0:T(128)} %bitcast.1.part_ref, s32[72]{0:T(128)S(1)} %get-tuple-element.20.meta_ref, bf16[3,3072,128]{2,1,0:T(8,128)(2,1)S(1)} %get-tuple-element.21.kv_ref, ...), custom_call_target="tpu_custom_call", output_to_operand_aliasing={{}: (11, {})} | custom-call | tf_op jit(solution)/shard_map/pallas_call | solution.py:806
  79.1 25.2 %all_to_all.11.w_ref = bf16[32,192,128]{2,1,0:T(8,128)(2,1)S(1)} all-to-all(bf16[32,192,128]{2,1,0:T(8,128)(2,1)S(1)} %shard_map.90), channel_id=1, replica_groups=mesh['grp'=4,'blk'=32] {'blk'}, dimensions={0} | all-to-all | bytes 3145728 | tf_op jit(solution)/shard_map/all_to_all | solution.py:851
  104.3 1.4 %shard_map.91 = (f32[168,512]{1,0:T(8,128)}, f32[168,512]{1,0:T(8,128)}, f32[168,512]{1,0:T(8,128)}) custom-call(s32[1]{0:T(128)} %bitcast.group_ref, bf16[32,192,128]{2,1,0:T(8,128)(2,1)S(1)} %all_to_all.11.w_ref), custom_call_target="tpu_custom_call" | custom-call | tf_op jit(solution)/shard_map/pallas_call | solution.py:853
Async XLA Ops:
  44.9 4.6 %collective-permute-start = (bf16[560,128]{1,0:T(8,128)(2,1)S(1)}, bf16[560,128]{1,0:T(8,128)(2,1)S(1)}, u32[]{:S(2)}, u32[]{:S(2)}) collective-permute-start(bf16[560,128]{1,0:T(8,128)(2,1)S(1)} %get-tuple-element.23.m0_in), channel_id=1, source_target_pairs={{96,16},{97,17},{98,18},{99,19},{100,20},{101,21},{102,22},{103,23... | collective-permute-start | bytes 430088 | tf_op jit(solution)/shard_map/ppermute | solution.py:845
  46.2 3.6 %collective-permute-start.1 = (bf16[560,128]{1,0:T(8,128)(2,1)S(1)}, bf16[560,128]{1,0:T(8,128)(2,1)S(1)}, u32[]{:S(2)}, u32[]{:S(2)}) collective-permute-start(bf16[560,128]{1,0:T(8,128)(2,1)S(1)} %get-tuple-element.24.m1_in), channel_id=1, source_target_pairs={{96,48},{97,49},{98,50},{99,51},{100,52},{101,53},{102,54},{103,55... | collective-permute-start | bytes 430088 | tf_op jit(solution)/shard_map/ppermute | solution.py:845
  47.5 2.3 %collective-permute-start.2 = (bf16[560,128]{1,0:T(8,128)(2,1)S(1)}, bf16[560,128]{1,0:T(8,128)(2,1)S(1)}, u32[]{:S(2)}, u32[]{:S(2)}) collective-permute-start(bf16[560,128]{1,0:T(8,128)(2,1)S(1)} %get-tuple-element.25.m2_in), channel_id=1, source_target_pairs={{96,64},{97,65},{98,66},{99,67},{100,68},{101,69},{102,70},{103,71... | collective-permute-start | bytes 430088 | tf_op jit(solution)/shard_map/ppermute | solution.py:845
  50.7 15.5 %collective-permute-start.5 = (bf16[544,128]{1,0:T(8,128)(2,1)S(1)}, bf16[544,128]{1,0:T(8,128)(2,1)S(1)}, u32[]{:S(2)}, u32[]{:S(2)}) collective-permute-start(bf16[544,128]{1,0:T(8,128)(2,1)S(1)} %get-tuple-element.32), channel_id=1, source_target_pairs={{64,96},{65,97},{66,98},{67,99},{68,100},{69,101},{70,102},{71,103... | collective-permute-start | bytes 417800 | tf_op jit(solution)/shard_map/ppermute | solution.py:848
  52.0 14.2 %collective-permute-start.4 = (bf16[544,128]{1,0:T(8,128)(2,1)S(1)}, bf16[544,128]{1,0:T(8,128)(2,1)S(1)}, u32[]{:S(2)}, u32[]{:S(2)}) collective-permute-start(bf16[544,128]{1,0:T(8,128)(2,1)S(1)} %get-tuple-element.32), channel_id=1, source_target_pairs={{48,96},{49,97},{50,98},{51,99},{52,100},{53,101},{54,102},{55,103... | collective-permute-start | bytes 417800 | tf_op jit(solution)/shard_map/ppermute | solution.py:848
  53.3 15.8 %collective-permute-start.3 = (bf16[544,128]{1,0:T(8,128)(2,1)S(1)}, bf16[544,128]{1,0:T(8,128)(2,1)S(1)}, u32[]{:S(2)}, u32[]{:S(2)}) collective-permute-start(bf16[544,128]{1,0:T(8,128)(2,1)S(1)} %get-tuple-element.32), channel_id=1, source_target_pairs={{16,96},{17,97},{18,98},{19,99},{20,100},{21,101},{22,102},{23,103... | collective-permute-start | bytes 417800 | tf_op jit(solution)/shard_map/ppermute | solution.py:848
